TPU v7x, 128 devices: a whole 4x4x4 slice. The times are simulated.
128 devices in a mesh: ha: 128 (over y, x, z, core).
Axes of the slice: x: 4, y: 4, z: 4, core: 2. Of those that a mesh axis runs over, the one named last changes fastest.
Arguments:
- density: float32 [4096, 18432], P('ha'), may hold values from -6 to 6
- up_link: int32 [4096, 40], P('ha'), may hold values from -1 to 4095, as said below
- down_link: int32 [4096, 40], P('ha'), may hold values from -1 to 4095, as said below
- occupation: int32 [4096, 40], P('ha'), may hold values from 0 to 3, as said below
- pigments: int32 [40], replicated, may hold values from 0 to 95
- hamiltonian: float32 [96, 96], replicated, as said below
- dipole: float32 [96, 96], replicated, as said below
- damping_rates: float32 [40], replicated, may hold values from 0.05 to 0.5
- coupling_re: float32 [40], replicated, may hold values from 0.3 to 1.5
- coupling_im: float32 [40], replicated, may hold values from -1 to 1
- field: float32 [64], replicated, may hold values from -1.5 to 1.5
- pulse_steps: int32 [2], replicated, may hold values from 0 to 63
Outputs:
- evolved: float32 [4096, 18432], P('ha')
Inputs may be any that keep to these rules, and one draw needn't show every extreme that they name: The auxiliaries are the occupation vectors over the 40 modes whose occupations sum to at most 3: in a fixed order of the modes, the first 4096 of them taken by total occupation and then lexicographically. The p-th of them lies on device sigma(p mod 128), at a slot of that device, with sigma a permutation of the devices; the slots and the labels of the modes are permuted as well. up_link[a, k] is the auxiliary with occupation of mode k raised by one if that one is among them, else -1 (always -1 where the total is 3). `down_link`: the auxiliary with occupation of mode k lowered by one, -1 where that occupation is 0; the inverse of up_link. `occupation`: each row sums to at most 3. `hamiltonian`: Symmetric, diagonal energies of order one and off-diagonal couplings. `dipole`: Symmetric.
All inputs are finite; a program needn't handle non-finite values.
Results may differ from a plain program's by a relative error of at most 0.0003.
Values sent between devices are 32-bit elements; how exact they have to be, the bound alone decides.
No kernel may reach another device: no remote copies, remote signals or barrier semaphores. Data moves between devices by JAX's collectives and lax.ppermute only.
A program may use at most 128 MiB of HBM per device.

v0:
```python
import functools
from typing import NamedTuple

import jax
import jax.numpy as jnp
from jax import lax
from jax.experimental import pallas as pl
from jax.experimental.pallas import tpu as pltpu
from jax.sharding import PartitionSpec as P

M = 96
K = 40
A = 32
N = 128
Q = A * K
ROWS = 97
LIST = 192
WIDE = 512
TAG = 96
CALL = 2048
PART = A // 4
HALF = 0.05
STEP = 0.1


class Size(NamedTuple):
    slots: int
    group: int
    forward: int
    few: int
    unroll: int

    @property
    def relay(self):
        return self.group * self.forward

    @property
    def pieces(self):
        return 3 * self.slots + 1

    @property
    def factor(self):
        return -(-6 * self.few // 128) * 128


EVERY = Size(8, 8, 8, 8, 1)
MOST = Size(4, 16, 8, 32, 8)

f32, bf16, i32 = jnp.float32, jnp.bfloat16, jnp.int32
VMEM = pl.BlockSpec(memory_space=pltpu.VMEM)
SMEM = pl.BlockSpec(memory_space=pltpu.SMEM)
HBM = pl.BlockSpec(memory_space=pltpu.HBM)
NT = (((1,), (1,)), ((), ()))


def iota(shape, axis):
    return lax.broadcasted_iota(i32, shape, axis)


def dot(a, b):
    return jnp.dot(a, b, preferred_element_type=f32)


def dot_nt(a, b):
    return lax.dot_general(a, b, NT, preferred_element_type=f32)


def split(x):
    high = x.astype(bf16)
    return high, (x - high.astype(f32)).astype(bf16)


def pick(ones, x):
    high, low = split(x)
    return dot(ones, high) + dot(ones, low)


def onehot(mask):
    return jnp.where(mask, 1.0, 0.0).astype(bf16)


def shift(x, bits):
    return lax.shift_right_arithmetic(x, bits)


def widen(o0, o1, o2):
    lane = iota(o0.shape, 1)
    keep = lane < M
    t1 = pltpu.roll(jnp.where(lane >= 96, o0, o1), 32, 1)
    t2 = pltpu.roll(jnp.where(lane >= 64, o1, o2), 64, 1)
    t3 = pltpu.roll(o2, 96, 1)
    return [jnp.where(keep, t, 0.0) for t in (o0, t1, t2, t3)]


def narrow(t0, t1, t2, t3):
    lane = iota(t0.shape, 1)
    r1, r2, r3 = pltpu.roll(t1, 96, 1), pltpu.roll(t2, 64, 1), pltpu.roll(t3, 32, 1)
    return jnp.where(lane < 96, t0, r1), jnp.where(lane < 64, r1, r2), jnp.where(lane < 32, r2, r3)


def tile(x, j):
    return x[:, j * 128 : (j + 1) * 128]


def pigment_lanes(pig):
    lane = iota((1, 128), 1)
    at = jnp.concatenate([pig[...], jnp.full((1, 128 - K), -1, i32)], axis=1)
    again = pltpu.roll(at, K, 1) + 128
    return jnp.where(lane < K, at, jnp.where(lane < 2 * K, again, -1))


def pigment_rows(pig):
    at = jnp.broadcast_to(pigment_lanes(pig).astype(f32), (128, 128)).T[0 : 2 * K, 0:1]
    return jnp.where(iota((2 * K, 256), 1) == at.astype(i32), 1.0, 0.0)


def each(start, stop, unroll, body):
    def step(i, carry):
        body(i)
        return carry

    if unroll >= stop - start:
        for i in range(start, stop):
            body(i)
    else:
        lax.fori_loop(start, stop, step, 0, unroll=unroll)


def lanes(first):
    return pl.ds(pl.multiple_of(first, 128) if not isinstance(first, int) else first, 128)


def aux(ref, a):
    rows = pl.ds(a * ROWS, M)
    return jnp.concatenate([ref[0, rows, :], ref[1, rows, :]], axis=1)


def store_aux(ref, a, x):
    rows = pl.ds(a * ROWS, M)
    ref[0, rows, :] = x[:, 0:128]
    ref[1, rows, :] = x[:, 128:256]


def parts(source, target, sem):
    copies = []
    for j in range(A // PART):
        rows = pl.ds(j * PART * ROWS, PART * ROWS)
        copies.append(pltpu.make_async_copy(source.at[:, rows, :], target.at[:, rows, :], sem.at[j]))
    return copies


def plan(size, raw, listed, slots):
    flat = [jnp.zeros((8, 128), f32) for _ in range(5)]
    lane = iota((8, 128), 1)
    for b in range(16):
        piece = raw[pl.ds(b, 8, stride=16), :]
        first, at = divmod(b * K, 128)
        turned = pltpu.roll(piece, at, 1) if at else piece
        flat[first] = jnp.where((lane >= at) & (lane < at + K), turned, flat[first])
        if at + K > 128:
            flat[first + 1] = jnp.where(lane < at + K - 128, turned, flat[first + 1])
    flat = jnp.concatenate(flat, axis=1)
    before = onehot(iota((256, 256), 0) < iota((256, 256), 1))
    carry = jnp.zeros((N, 1), f32)
    facts = jnp.zeros((8, LIST), f32)
    for h in range(2):
        for g in range(2):
            row = slice(2 * h + g, 2 * h + g + 1)
            for low, width in ((0, 256), (256, 256), (512, 128)):
                span = slice(low, low + width)
                link = flat[row, span].astype(i32)
                dest = shift(link, 5)
                mine = dest == iota((N, width), 0)
                ones = jnp.where(mine, 1.0, 0.0)
                count = dot(ones.astype(bf16), before[0:width, 0:width]) + carry
                carry = count[:, width - 1 : width] + ones[:, width - 1 : width]
                rank = jnp.sum(jnp.where(mine, count, 0.0), axis=0, keepdims=True)
                place = jnp.sum(count, axis=0, keepdims=True).astype(i32)
                place = jnp.where(link >= 0, place, -1)
                item = iota((1, width), 1) + low
                mode = item - K * shift(item * 1639, 16)
                tag = ((link & 31) * K + mode + 1).astype(f32)
                if h == 0:
                    raised = flat[4 + g : 5 + g, span] + 1.0
                    sa, sb = raised * flat[6:7, span], raised * flat[7:8, span]
                else:
                    sa, sb = jnp.ones((1, width), f32), jnp.zeros((1, width), f32)
                here = onehot(iota((LIST, width), 0) == place)
                column = pl.ds(g * 640 + low, width)
                listed[:, column] = here if h == 0 else listed[:, column] + here
                fact = jnp.concatenate(
                    [rank, tag, sa, sb, dest.astype(f32), jnp.zeros((3, width), f32)], axis=0
                )
                high, low_part = split(fact)
                facts += dot_nt(high, here) + dot_nt(low_part, here)
    rank, tag, dest = facts[0:1], facts[1:2], facts[4:5]
    goal = dest.astype(i32)
    bits = size.group.bit_length() - 1
    me = lax.axis_index("ha")
    rows, columns = iota((N, N), 0), iota((N, N), 1)
    mate = shift(rows, bits) == shift(columns, bits)
    first = ((columns - me) & (size.group - 1)) < ((rows - me) & (size.group - 1))
    level = iota((N, 128), 1)
    free = onehot((carry <= level.astype(f32)) & (level < size.slots))
    here = dot(onehot(mate & first), free)
    whole = dot(onehot(mate), free)
    over = jnp.broadcast_to(jnp.maximum(carry - size.slots, 0.0), (N, 128)).astype(bf16)
    over_before = dot(onehot(mate & (columns < rows)), over)[:, 0:1]
    device = iota((N, LIST), 0)
    turn = jnp.sum(jnp.where(device == goal, over_before, 0.0), axis=0, keepdims=True) + rank - size.slots
    near = shift(device, bits) == shift(goal, bits)
    via_slot = jnp.full((N, LIST), -1.0, f32)
    ahead = jnp.zeros((N, 1), f32)
    for r in range(size.slots):
        hit = near & (carry <= r) & (here[:, r : r + 1] + ahead == turn)
        via_slot = jnp.where(hit, r * N + device.astype(f32), via_slot)
        ahead = ahead + whole[:, r : r + 1]
    via_slot = jnp.max(via_slot, axis=0, keepdims=True)
    past = rank >= size.slots
    lost = jnp.max(jnp.where(past & (via_slot < 0.0), 1.0, 0.0), axis=1, keepdims=True)
    slot = jnp.where(past, via_slot, rank * N + dest)
    slot = jnp.where(tag == 0.0, -1.0, slot)
    tag = jnp.where(past, tag + CALL * (1 + (goal & (size.group - 1))).astype(f32), tag)
    lost = jnp.broadcast_to(lost, (1, LIST))
    slots[...] = jnp.concatenate([slot, tag, facts[2:4], lost, jnp.zeros((3, LIST), f32)], axis=0)


def items(a):
    return pl.ds(a * K if isinstance(a, int) else pl.multiple_of(a * K, 8), K)


def table_aux(x, rows, a, table):
    high, low = split(x)
    ones = rows[0:K, 0:M]
    row = dot(ones, high) + dot(ones, low)
    blank = jnp.zeros((128 - M, 256), bf16)
    high, low = jnp.concatenate([high, blank], axis=0), jnp.concatenate([low, blank], axis=0)
    column = dot_nt(rows, high) + dot_nt(rows, low)
    here = items(a)
    table[0, here, :] = row[:, 0:128]
    table[1, here, :] = row[:, 128:256]
    table[2, here, :] = column[0:K]
    table[3, here, :] = column[K : 2 * K]


def fill(size, table, listed, slots, lost, send):
    message = pick(listed[...], jnp.concatenate([table[j] for j in range(4)], axis=1))
    info = jnp.concatenate([slots[...], jnp.zeros((120, LIST), f32)], axis=0).T
    tag, sa, sb = info[:, 1:2], info[:, 2:3], info[:, 3:4]
    x0, x1, x2, x3 = (tile(message, j) for j in range(4))
    x0, x1, x2, x3 = sa * x1 + sb * x0, sb * x1 - sa * x0, sb * x2 - sa * x3, sa * x2 + sb * x3
    x0 = jnp.where(iota((LIST, 128), 1) == TAG, tag, x0)
    high, low = split(jnp.concatenate([x0, x1, x2, x3], axis=1))
    goal = slots[0:1, :].astype(i32)
    lane = iota((N, 128), 1)
    tags = jnp.where(lane == size.slots, lost, 0.0)
    for r in range(size.slots):
        ones = onehot(iota((N, LIST), 0) + r * N == goal)
        part = dot(ones, high) + dot(ones, low)
        tags = jnp.where(lane == r, pltpu.roll(tile(part, 0), (r - TAG) % 128, 1), tags)
        for j, piece in enumerate(narrow(*(tile(part, j) for j in range(4)))):
            send[pl.ds(3 * r + j, N, stride=size.pieces), :] = piece
    send[pl.ds(size.pieces - 1, N, stride=size.pieces), :] = tags


def open_kernel(
    size, pig, real, imaginary, up, down, level, density,
    out, send, listing, slots,
    state, listed, held, table, raw, leave, sem,
):
    copy = pltpu.make_async_copy(density, held, sem.at[0])
    copy.start()
    raw[...] = jnp.zeros((128, 128), f32)
    raw[0:32, 0:K] = up[...].astype(f32)
    raw[32:64, 0:K] = down[...].astype(f32)
    raw[64:96, 0:K] = level[...].astype(f32)
    raw[96:112, 0:K] = jnp.broadcast_to(real[...], (16, K))
    raw[112:128, 0:K] = jnp.broadcast_to(imaginary[...], (16, K))
    plan(size, raw, listed, slots)
    note = pltpu.make_async_copy(listed, listing, sem.at[1])
    note.start()
    rows = pigment_rows(pig).astype(bf16)
    copy.wait()

    def unfold(m):
        pieces = widen(*(held[:, lanes(m * 384 + j * 128)] for j in range(3)))
        for j in range(2):
            for h in range(2):
                state[h, pl.ds(2 * m + j, A, stride=ROWS), :] = pieces[2 * j + h]

    each(0, M // 2, size.unroll, unfold)
    give = parts(state, out, leave)
    for copy in give:
        copy.start()
    each(0, A, size.unroll, lambda a: table_aux(aux(state, a), rows, a, table))
    fill(size, table, listed, slots, jnp.zeros((1, 1), f32), send)
    note.wait()
    for copy in give:
        copy.wait()


def commutator_kernel(
    unroll, section, scale, field, steps, rates, level, hamiltonian, dipole, first, now,
    base, start, x, out, twice, fading, arrive, also, leave,
):
    fetch, more = parts(now, x, arrive), parts(first, start, also)
    for copy in fetch + more:
        copy.start()
    h = hamiltonian[...] + field[steps[section]] * dipole[...]
    twice[...] = jnp.zeros((256, 256), f32)
    twice[0:M, 0:M] = h
    twice[128 : 128 + M, 128 : 128 + M] = h
    hh, hl = split(h)
    bh, bl = split(twice[...])
    decay = jnp.sum(level[...].astype(f32) * rates[...], axis=1, keepdims=True)
    fading[...] = jnp.broadcast_to(decay, (A, 128))
    give = parts(out, base, leave)

    def one(a):
        y = aux(x, a)
        yh, yl = split(y)
        left = dot(hh, yh) + dot(hl, yh) + dot(hh, yl)
        right = dot(yh, bh) + dot(yh, bl) + dot(yl, bh)
        d = left - right
        d = jnp.concatenate([d[:, 128:256], -d[:, 0:128]], axis=1) - fading[pl.ds(a, 1), 0:1] * y
        store_aux(out, a, aux(start, a) + scale * d)

    for j in range(A // PART):
        fetch[j].wait()
        more[j].wait()
        each(j * PART, (j + 1) * PART, unroll, one)
        give[j].start()
    for copy in give:
        copy.wait()


def receive_kernel(size, got, mine, relay, lost, high, low, ones):
    tags = got[pl.ds(size.pieces - 1, N, stride=size.pieces), :]
    across = tags.T[0:16, :].astype(i32)
    failed = jnp.max(across[size.slots : size.slots + 1], axis=1, keepdims=True)
    across = across[0 : size.slots]
    lane = iota((N, 128), 1)
    for r in range(size.slots):
        rows = pl.ds(r * N, N)
        t0, t1, t2, t3 = widen(*(got[pl.ds(3 * r + j, N, stride=size.pieces), :] for j in range(3)))
        t0 = jnp.where(lane == TAG, pltpu.roll(tags, TAG - r, 1), t0)
        for j, t in enumerate((t0, t1, t2, t3)):
            h, l = split(t)
            high[rows, j * 128 : (j + 1) * 128] = h
            low[rows, j * 128 : (j + 1) * 128] = l
    kinds = -(-(size.group + 1) // 8) * 8
    height = size.slots * kinds
    spread = [jnp.broadcast_to(across[r : r + 1], (kinds, N)) for r in range(size.slots)]
    spread = jnp.concatenate(spread, axis=0)
    kind = iota((height, N), 0) % kinds
    flags = (spread > 0) & (shift(spread, 11) == kind)
    ones_at = onehot(flags)
    before = onehot(iota((N, N), 0) < iota((N, N), 1))
    count = dot(ones_at, before)
    total = dot(ones_at, jnp.ones((N, N), bf16))
    rows, columns = iota((height, height), 0), iota((height, height), 1)
    earlier = onehot((rows % kinds == columns % kinds) & (columns < rows))
    count = count + dot(earlier, total.astype(bf16))
    member = count < jnp.where(kind == 0, LIST, size.forward).astype(f32)
    failed = jnp.maximum(failed, jnp.max(jnp.where(flags & ~member, 1.0, 0.0)).astype(i32))
    first = jnp.where(kind == 0, 0, LIST + (kind - 1) * size.forward)
    place = jnp.where(flags & member, count + first.astype(f32), -1.0)
    order = iota((LIST + size.relay, 128), 0)
    for r in range(size.slots):
        here = jnp.max(place[r * kinds : (r + 1) * kinds], axis=0, keepdims=True).astype(i32)
        ones[:, r * N : (r + 1) * N] = onehot(order == here)
    lost[...] = jnp.broadcast_to(failed, (8, 128))
    out = dot(ones[...], high[...]) + dot(ones[...], low[...])
    mine[...] = out[0:LIST]
    out = out[LIST:]
    called = CALL * (iota((size.relay, WIDE), 0) // size.forward + 1).astype(f32)
    mark = (iota((size.relay, WIDE), 1) == TAG) & (out > 0.0)
    relay[...] = out - jnp.where(mark, called, 0.0)


def clear(message, scale):
    return jnp.where((iota(message.shape, 1) & 127) < M, message * scale, 0.0)


def place_kernel(unroll, scale, pig, mine, base, out, total, dense, arrive, leave):
    fetch = parts(base, total, arrive)
    for copy in fetch:
        copy.start()
    rows = pigment_rows(pig)
    rowsb = rows.astype(bf16)
    rowst = jnp.concatenate([rows[0:K, 0:128], jnp.zeros((128 - K, 128), f32)], axis=0).T
    rowst = rowst[0:M, 0:K].astype(bf16)
    message = mine[...]
    tag = message[:, 0:128].T[TAG : TAG + 1, :].astype(i32)
    placed = pick(onehot(iota((Q, LIST), 0) + 1 == tag), clear(message, scale))
    for j in range(4):
        dense[j] = tile(placed, j)
    blank = jnp.zeros((128 - 2 * K, 128), f32)
    give = parts(total, out, leave)

    def one(a):
        here = items(a)
        row = jnp.concatenate([dense[0, here, :], dense[1, here, :]], axis=1)
        high, low = split(row)
        new = dot(rowst, high) + dot(rowst, low)
        column = jnp.concatenate([dense[2, here, :], dense[3, here, :], blank], axis=0).T
        high, low = split(column[0:M, 0 : 2 * K])
        new = new + dot(high, rowsb) + dot(low, rowsb)
        store_aux(total, a, aux(total, a) + new)

    for j in range(A // PART):
        fetch[j].wait()
        each(j * PART, (j + 1) * PART, unroll, one)
        give[j].start()
    for copy in give:
        copy.wait()


def few(size, pig, scale, relay):
    message = relay[...]
    head = message[:, 0:128]
    if size.relay < 128:
        head = jnp.concatenate([head, jnp.zeros((128 - size.relay, 128), f32)], axis=0)
    tag = head.T[TAG : TAG + 1, 0 : size.relay]
    flag = jnp.where(tag > 0.5, 1.0, 0.0)
    before = onehot(iota((size.relay, size.relay), 0) < iota((size.relay, size.relay), 1))
    place = dot(jnp.broadcast_to(flag, (8, size.relay)).astype(bf16), before)[0:1, :]
    place = jnp.where(tag > 0.5, place, -1.0).astype(i32)
    message = pick(onehot(iota((size.few, size.relay), 0) == place), message)
    tag = message[:, TAG : TAG + 1].astype(i32)
    message = clear(message, scale)
    who = shift((tag - 1) * 1639, 16)
    who = jnp.where(tag > 0, who, -1)
    mode = tag - 1 - who * K
    lane = iota((size.few, 128), 1)
    at = jnp.sum(jnp.where(lane == mode, pigment_lanes(pig), 0).astype(f32), axis=1, keepdims=True)
    at = at.astype(i32)
    ones = jnp.where(lane == at, 1.0, 0.0)
    zero = jnp.zeros((size.few, 128), f32)
    high = message.astype(bf16).astype(f32)
    low = message - high
    rest = size.factor - 6 * size.few
    left = [ones, ones, tile(high, 2), tile(low, 2), tile(high, 3), tile(low, 3), jnp.zeros((rest, 128), f32)]
    left = jnp.concatenate(left, axis=0)
    owner = jnp.concatenate([who.astype(f32)] * 6 + [jnp.full((rest, 1), -1.0, f32)], axis=0)
    left = jnp.where(iota((size.factor, 128), 1) == M, owner, left).T
    real = jnp.concatenate([ones, zero], axis=1)
    imaginary = jnp.concatenate([zero, ones], axis=1)
    right = [high[:, 0:256], low[:, 0:256], real, real, imaginary, imaginary, jnp.zeros((rest, 256), f32)]
    right = jnp.concatenate(right, axis=0)
    return left[0:M], left[M : M + 1].astype(i32), right.astype(bf16)


def add_few(ref, j, left, whom, right):
    span = range(j * PART, (j + 1) * PART)
    factors = jnp.concatenate([jnp.where(whom == a, left, 0.0).astype(bf16) for a in span], axis=0)
    new = dot(factors, right)
    for n, a in enumerate(span):
        store_aux(ref, a, aux(ref, a) + new[n * M : (n + 1) * M])


def middle_kernel(
    size, pig, relay, partial, listed, slots, lost, out, send, middle, table, chosen, arrive, leave, other
):
    fetch = parts(partial, middle, arrive)
    for copy in fetch:
        copy.start()
    choose = pltpu.make_async_copy(listed, chosen, other)
    choose.start()
    factors = few(size, pig, HALF, relay)
    rows = pigment_rows(pig).astype(bf16)
    give = parts(middle, out, leave)
    for j in range(A // PART):
        fetch[j].wait()
        add_few(middle, j, *factors)
        give[j].start()
        each(j * PART, (j + 1) * PART, size.unroll, lambda a: table_aux(aux(middle, a), rows, a, table))
    choose.wait()
    fill(size, table, chosen, slots, jnp.maximum(slots[4:5, 0:1], lost[0:1, 0:1].astype(f32)), send)
    for copy in give:
        copy.wait()


def close_kernel(size, pig, relay, partial, out, total, matrix, arrive, leave):
    fetch = parts(partial, total, arrive)
    for copy in fetch:
        copy.start()
    factors = few(size, pig, STEP, relay)
    give = []
    for j in range(A // PART):
        fetch[j].wait()
        add_few(total, j, *factors)
        span = pl.ds(j * PART, PART)

        def fold(m):
            pieces = []
            for i in range(2):
                for h in range(2):
                    pieces.append(total[h, pl.ds(j * PART * ROWS + 2 * m + i, PART, stride=ROWS), :])
            for i, piece in enumerate(narrow(*pieces)):
                matrix[span, lanes(m * 384 + i * 128)] = piece

        each(0, M // 2, size.unroll, fold)
        give.append(pltpu.make_async_copy(matrix.at[span, :], out.at[span, :], leave.at[j]))
        give[j].start()
    for copy in give:
        copy.wait()


def call(kernel, in_specs, outs, scratch, out_specs):
    return pl.pallas_call(
        kernel,
        in_specs=in_specs,
        out_specs=out_specs,
        out_shape=[jax.ShapeDtypeStruct(*o) for o in outs],
        scratch_shapes=[s if not isinstance(s, tuple) else pltpu.VMEM(*s) for s in scratch],
        compiler_params=pltpu.CompilerParams(vmem_limit_bytes=60 * 1024 * 1024),
    )


def on_device(
    density,
    up_link,
    down_link,
    occupation,
    pigments,
    hamiltonian,
    dipole,
    damping_rates,
    coupling_re,
    coupling_im,
    field,
    pulse_steps,
):
    big = ((2, A * ROWS, 128), f32)
    listing = ((LIST, Q), bf16)
    dense = ((4, Q, 128), f32)
    sems = pltpu.SemaphoreType.DMA((A // PART,))
    pig = pigments.reshape(1, K)

    def begin(size):
        return call(
            functools.partial(open_kernel, size),
            [VMEM] * 6 + [HBM],
            [big, ((N * size.pieces, 128), f32), listing, ((8, LIST), f32)],
            [
                big,
                listing,
                ((A, 2 * M * M), f32),
                dense,
                ((128, 128), f32),
                sems,
                pltpu.SemaphoreType.DMA((2,)),
            ],
            [HBM, VMEM, HBM, VMEM],
        )(
            pig,
            coupling_re.reshape(1, K),
            coupling_im.reshape(1, K),
            up_link,
            down_link,
            occupation,
            density,
        )

    def step(size, section, scale, state, x, send):
        got = lax.all_to_all(
            send.reshape(N, 1, size.pieces * 128), "ha", split_axis=0, concat_axis=0, tiled=True
        )
        base = call(
            functools.partial(commutator_kernel, min(size.unroll, 2), section, scale),
            [SMEM, SMEM] + [VMEM] * 4 + [HBM] * 2,
            [big],
            [big, big, big, ((256, 256), f32), ((A, 128), f32), sems, sems, sems],
            [HBM],
        )(field, pulse_steps, damping_rates.reshape(1, K), occupation, hamiltonian, dipole, state, x)[0]
        got, base = lax.optimization_barrier((got, base))
        ahead = ((size.slots * N, WIDE), bf16)
        mine, relay, lost = call(
            functools.partial(receive_kernel, size),
            [VMEM],
            [((LIST, WIDE), f32), ((size.relay, WIDE), f32), ((8, 128), i32)],
            [ahead, ahead, ((LIST + size.relay, size.slots * N), bf16)],
            [VMEM, VMEM, VMEM],
        )(got.reshape(N * size.pieces, 128))
        relay = lax.all_to_all(
            relay.reshape(size.group, size.forward, WIDE),
            "ha",
            split_axis=0,
            concat_axis=0,
            tiled=True,
            axis_index_groups=[[i + j for j in range(size.group)] for i in range(0, N, size.group)],
        ).reshape(size.relay, WIDE)
        partial = call(
            functools.partial(place_kernel, min(size.unroll, 8), scale),
            [VMEM, VMEM, HBM],
            [big],
            [big, dense, sems, sems],
            [HBM],
        )(pig, mine, base)[0]
        return relay, partial, lost

    def finish(size, state, relay, partial, lost, listed, slots):
        middle, send = call(
            functools.partial(middle_kernel, size),
            [VMEM, VMEM, HBM, HBM, VMEM, VMEM],
            [big, ((N * size.pieces, 128), f32)],
            [big, dense, listing, sems, sems, pltpu.SemaphoreType.DMA],
            [HBM, VMEM],
        )(pig, relay, partial, listed, slots, lost)
        relay, partial, lost = step(size, 1, STEP, state, middle, send)
        return call(
            functools.partial(close_kernel, size),
            [VMEM, VMEM, HBM],
            [((A, 2 * M * M), f32)],
            [big, ((A, 2 * M * M), f32), sems, sems],
            [HBM],
        )(pig, relay, partial)[0], lost[0, 0]

    state, send, listed, slots = begin(MOST)
    relay, partial, lost = step(MOST, 0, HALF, state, state, send)

    def again():
        state, send, listed, slots = begin(EVERY)
        relay, partial, lost = step(EVERY, 0, HALF, state, state, send)
        return finish(EVERY, state, relay, partial, lost, listed, slots)[0]

    out, lost = finish(MOST, state, relay, partial, lost, listed, slots)

    return lax.cond(lost > 0, again, lambda: out)


def solution(mesh):
    rows = P("ha", None)
    return jax.shard_map(
        on_device,
        mesh=mesh,
        in_specs=(rows, rows, rows, rows) + (P(),) * 8,
        out_specs=rows,
        check_vma=False,
    )
```

profile of v0, /device:TPU:1, one launch (start us, length us, event | category | flops | bytes accessed | tf_op | source)
XLA Modules:
  0.0 107.1 jit_solution(5562993952963078510)
XLA Ops:
  0.0 0.0 copy-start.9
  0.0 0.0 copy-start.16
  0.0 0.0 copy-start.15
  0.0 0.0 copy-start.8
  0.0 0.0 copy-start.7
  0.0 0.0 copy-start.17
  0.0 9.0 %shard_map.120 = (f32[2,3104,128]{2,1,0:T(8,128)}, f32[1664,128]{1,0:T(8,128)}, bf16[192,1280]{1,0:T(8,128)(2,1)}, f32[8,192]{1,0:T(8,128)}) custom-call(s32[1,40]{1,0:T(1,128)} %bitcast.40, f32[1,40]{1,0:T(1,128)} %bitcast.50, f32[1,40]{1,0:T(1,128)} %bitcast.52, s32[32,40]{1,0:T(8,128)} %up.1, s32[32,40]{1,0:T(8,128)} %down.1, s32[32,40]{1,0:T(8,128)} %level.5, ...), custom_call_target="tpu_custom_call" | custom-call | tf_op jit(solution)/shard_map/pallas_call | solution.py:542
  9.1 11.5 %all-to-all-start.4 = ((f32[128,1,1664]{2,1,0:T(1,128)}), f32[128,1,1664]{2,1,0:T(1,128)S(1)}, u32[]{:S(2)}, u32[]{:S(2)}) async-start(f32[128,1,1664]{2,1,0:T(1,128)} %bitcast.33), calls=%async_computation.4 | async-start | bytes 1703936 | tf_op jit(solution)/shard_map/all_to_all | solution.py:567
  20.6 0.0 copy-done.9
  20.6 0.0 copy-done.16
  20.6 0.0 copy-done.15
  20.6 0.0 copy-done.8
  20.6 0.0 copy-done.7
  20.6 0.0 copy-done.17
  20.6 0.0 copy-start.14
  20.6 8.7 %shard_map.121.base = f32[2,3104,128]{2,1,0:T(8,128)} custom-call(f32[64]{0:T(128)S(1)} %copy-done.15, s32[2]{0:T(128)S(1)} %copy-done.16, f32[1,40]{1,0:T(1,128)S(1)} %bitcast.46, s32[32,40]{1,0:T(8,128)S(1)} %copy-done.9, f32[96,96]{1,0:T(8,128)S(1)} %copy-done.7, f32[96,96]{1,0:T(8,128)S(1)} %copy-done.8, f32[2,3104,128]{2,1,0:T(8,128)} %get-tuple-element.77.first.now, ...), custom_call_target="tpu_custom_call" | custom-call | tf_op jit(solution)/shard_map/pallas_call | solution.py:570
  29.4 8.2 %all-to-all-done.4 = f32[128,1,1664]{2,1,0:T(1,128)S(1)} async-done(((f32[128,1,1664]{2,1,0:T(1,128)}), f32[128,1,1664]{2,1,0:T(1,128)S(1)}, u32[]{:S(2)}, u32[]{:S(2)}) %all-to-all-start.4) | async-done | bytes 852000 | tf_op jit(solution)/shard_map/all_to_all | solution.py:567
  37.6 0.0 copy-start.4
  37.6 0.9 copy-done.4
  38.5 2.9 %shard_map.122 = (f32[192,512]{1,0:T(8,128)}, f32[128,512]{1,0:T(8,128)}, s32[8,128]{1,0:T(8,128)}) custom-call(f32[1664,128]{1,0:T(8,128)} %bitcast.27), custom_call_target="tpu_custom_call" | custom-call | tf_op jit(solution)/shard_map/pallas_call | solution.py:579
  41.4 4.5 %all-to-all-start.5 = ((f32[16,8,512]{2,1,0:T(8,128)}), f32[16,8,512]{2,1,0:T(8,128)S(1)}, u32[]{:S(2)}, u32[]{:S(2)}) async-start(f32[16,8,512]{2,1,0:T(8,128)} %bitcast.37), calls=%async_computation.5 | async-start | bytes 524288 | tf_op jit(solution)/shard_map/all_to_all | solution.py:586
  46.0 0.0 copy-done.14
  46.0 5.9 %shard_map.123.partial = f32[2,3104,128]{2,1,0:T(8,128)} custom-call(s32[1,40]{1,0:T(1,128)S(1)} %bitcast.41, f32[192,512]{1,0:T(8,128)} %get-tuple-element.80.mine, f32[2,3104,128]{2,1,0:T(8,128)} %shard_map.121.base), custom_call_target="tpu_custom_call" | custom-call | tf_op jit(solution)/shard_map/pallas_call | solution.py:594
  51.9 1.3 %all-to-all-done.5 = f32[16,8,512]{2,1,0:T(8,128)S(1)} async-done(((f32[16,8,512]{2,1,0:T(8,128)}), f32[16,8,512]{2,1,0:T(8,128)S(1)}, u32[]{:S(2)}, u32[]{:S(2)}) %all-to-all-start.5) | async-done | bytes 262176 | tf_op jit(solution)/shard_map/all_to_all | solution.py:586
  53.2 0.7 copy-done.6
  53.9 7.6 %shard_map.124 = (f32[2,3104,128]{2,1,0:T(8,128)}, f32[1664,128]{1,0:T(8,128)}) custom-call(s32[1,40]{1,0:T(1,128)S(1)} %bitcast.42, f32[128,512]{1,0:T(8,128)} %bitcast.31, f32[2,3104,128]{2,1,0:T(8,128)} %shard_map.123.partial, bf16[192,1280]{1,0:T(8,128)(2,1)} %get-tuple-element.82.listed, f32[8,192]{1,0:T(8,128)} %get-tuple-element.83.slots, ...), custom_call_target="tpu_custom_call" | custom-call | tf_op jit(solution)/shard_map/pallas_call | solution.py:604
  61.5 4.6 %all-to-all-start.6 = ((f32[128,1,1664]{2,1,0:T(1,128)}), f32[128,1,1664]{2,1,0:T(1,128)S(1)}, u32[]{:S(2)}, u32[]{:S(2)}) async-start(f32[128,1,1664]{2,1,0:T(1,128)} %bitcast.32), calls=%async_computation.6 | async-start | bytes 1703936 | tf_op jit(solution)/shard_map/all_to_all | solution.py:567
  66.1 8.6 %shard_map.125.base = f32[2,3104,128]{2,1,0:T(8,128)} custom-call(f32[64]{0:T(128)S(1)} %copy-done.15, s32[2]{0:T(128)S(1)} %copy-done.16, f32[1,40]{1,0:T(1,128)S(1)} %bitcast.47, s32[32,40]{1,0:T(8,128)S(1)} %copy-done.9, f32[96,96]{1,0:T(8,128)S(1)} %copy-done.7, f32[96,96]{1,0:T(8,128)S(1)} %copy-done.8, f32[2,3104,128]{2,1,0:T(8,128)} %get-tuple-element.77.first.now, ...), custom_call_target="tpu_custom_call" | custom-call | tf_op jit(solution)/shard_map/pallas_call | solution.py:570
  74.7 8.5 %all-to-all-done.6 = f32[128,1,1664]{2,1,0:T(1,128)S(1)} async-done(((f32[128,1,1664]{2,1,0:T(1,128)}), f32[128,1,1664]{2,1,0:T(1,128)S(1)}, u32[]{:S(2)}, u32[]{:S(2)}) %all-to-all-start.6) | async-done | bytes 852000 | tf_op jit(solution)/shard_map/all_to_all | solution.py:567
  83.1 0.9 copy-done.3
  84.0 2.9 %shard_map.126 = (f32[192,512]{1,0:T(8,128)}, f32[128,512]{1,0:T(8,128)}, s32[8,128]{1,0:T(8,128)}) custom-call(f32[1664,128]{1,0:T(8,128)} %bitcast.26), custom_call_target="tpu_custom_call" | custom-call | tf_op jit(solution)/shard_map/pallas_call | solution.py:579
  87.0 4.5 %all-to-all-start.7 = ((f32[16,8,512]{2,1,0:T(8,128)}), f32[16,8,512]{2,1,0:T(8,128)S(1)}, u32[]{:S(2)}, u32[]{:S(2)}) async-start(f32[16,8,512]{2,1,0:T(8,128)} %bitcast.36), calls=%async_computation.7 | async-start | bytes 524288 | tf_op jit(solution)/shard_map/all_to_all | solution.py:586
  91.5 1.2 %slice.3 = s32[1,1]{1,0:T(1,128)} slice(s32[8,128]{1,0:T(8,128)} %get-tuple-element.88), slice={[0:1], [0:1]} | slice | bytes 8 | tf_op jit(solution)/shard_map/slice | solution.py:618
  93.3 5.8 %shard_map.127.partial = f32[2,3104,128]{2,1,0:T(8,128)} custom-call(s32[1,40]{1,0:T(1,128)S(1)} %bitcast.43, f32[192,512]{1,0:T(8,128)} %get-tuple-element.90.mine, f32[2,3104,128]{2,1,0:T(8,128)} %shard_map.125.base), custom_call_target="tpu_custom_call" | custom-call | tf_op jit(solution)/shard_map/pallas_call | solution.py:594
  99.2 0.0 copy-start
  99.2 0.0 copy-start.12
  99.2 0.0 copy-start.13
  99.2 0.0 copy-start.18
  99.2 0.0 copy-start.19
  99.3 0.0 all-to-all-done.7
  99.3 0.0 copy-start.5
  99.3 0.7 copy-done.5
  100.0 6.9 %shard_map.128 = f32[32,18432]{1,0:T(8,128)} custom-call(s32[1,40]{1,0:T(1,128)S(1)} %bitcast.44, f32[128,512]{1,0:T(8,128)} %bitcast.30, f32[2,3104,128]{2,1,0:T(8,128)} %shard_map.127.partial), custom_call_target="tpu_custom_call" | custom-call | tf_op jit(solution)/shard_map/pallas_call | solution.py:612
  106.9 0.0 copy-done
  106.9 0.0 copy-done.12
  106.9 0.0 copy-done.13
  106.9 0.0 copy-done.18
  106.9 0.0 copy-done.19
  (3 shorter events, 0.0 us)
Async XLA Ops:
  0.0 20.6 %copy-start.9 = (s32[32,40]{1,0:T(8,128)S(1)}, s32[32,40]{1,0:T(8,128)}, u32[]{:S(2)}) copy-start(s32[32,40]{1,0:T(8,128)} %level.5) | copy-start | bytes 15364
  0.0 20.6 %copy-start.16 = (s32[2]{0:T(128)S(1)}, s32[2]{0:T(128)}, u32[]{:S(2)}) copy-start(s32[2]{0:T(128)} %steps.3) | copy-start | bytes 28
  0.0 20.6 %copy-start.15 = (f32[64]{0:T(128)S(1)}, f32[64]{0:T(128)}, u32[]{:S(2)}) copy-start(f32[64]{0:T(128)} %field.3) | copy-start | bytes 772
  0.0 20.6 %copy-start.8 = (f32[96,96]{1,0:T(8,128)S(1)}, f32[96,96]{1,0:T(8,128)}, u32[]{:S(2)}) copy-start(f32[96,96]{1,0:T(8,128)} %dipole.3) | copy-start | bytes 110596
  0.0 20.6 %copy-start.7 = (f32[96,96]{1,0:T(8,128)S(1)}, f32[96,96]{1,0:T(8,128)}, u32[]{:S(2)}) copy-start(f32[96,96]{1,0:T(8,128)} %hamiltonian.3) | copy-start | bytes 110596
  0.0 20.6 %copy-start.17 = (f32[40]{0:T(128)S(1)}, f32[40]{0:T(128)}, u32[]{:S(2)}) copy-start(f32[40]{0:T(128)} %param.21) | copy-start | bytes 484
  9.1 28.6 %all-to-all-start.4 = ((f32[128,1,1664]{2,1,0:T(1,128)}), f32[128,1,1664]{2,1,0:T(1,128)S(1)}, u32[]{:S(2)}, u32[]{:S(2)}) async-start(f32[128,1,1664]{2,1,0:T(1,128)} %bitcast.33), calls=%async_computation.4 | async-start | bytes 1703936 | tf_op jit(solution)/shard_map/all_to_all | solution.py:567
  20.6 25.3 %copy-start.14 = (s32[40]{0:T(128)S(1)}, s32[40]{0:T(128)}, u32[]{:S(2)}) copy-start(s32[40]{0:T(128)} %param.18) | copy-start | bytes 484
  37.6 0.9 copy-start.4
  41.4 11.8 %all-to-all-start.5 = ((f32[16,8,512]{2,1,0:T(8,128)}), f32[16,8,512]{2,1,0:T(8,128)S(1)}, u32[]{:S(2)}, u32[]{:S(2)}) async-start(f32[16,8,512]{2,1,0:T(8,128)} %bitcast.37), calls=%async_computation.5 | async-start | bytes 524288 | tf_op jit(solution)/shard_map/all_to_all | solution.py:586
  53.2 0.7 copy-start.6
  61.5 21.6 %all-to-all-start.6 = ((f32[128,1,1664]{2,1,0:T(1,128)}), f32[128,1,1664]{2,1,0:T(1,128)S(1)}, u32[]{:S(2)}, u32[]{:S(2)}) async-start(f32[128,1,1664]{2,1,0:T(1,128)} %bitcast.32), calls=%async_computation.6 | async-start | bytes 1703936 | tf_op jit(solution)/shard_map/all_to_all | solution.py:567
  83.1 0.9 copy-start.3
  87.0 12.3 %all-to-all-start.7 = ((f32[16,8,512]{2,1,0:T(8,128)}), f32[16,8,512]{2,1,0:T(8,128)S(1)}, u32[]{:S(2)}, u32[]{:S(2)}) async-start(f32[16,8,512]{2,1,0:T(8,128)} %bitcast.36), calls=%async_computation.7 | async-start | bytes 524288 | tf_op jit(solution)/shard_map/all_to_all | solution.py:586
  99.2 7.7 %copy-start = (f32[32,18432]{1,0:T(8,128)S(1)}, f32[32,18432]{1,0:T(8,128)}, u32[]{:S(2)}) copy-start(f32[32,18432]{1,0:T(8,128)} %density.1) | copy-start | bytes 7077892
  99.2 7.7 %copy-start.12 = (s32[32,40]{1,0:T(8,128)S(1)}, s32[32,40]{1,0:T(8,128)}, u32[]{:S(2)}) copy-start(s32[32,40]{1,0:T(8,128)} %up.1) | copy-start | bytes 15364
  99.2 7.7 %copy-start.13 = (s32[32,40]{1,0:T(8,128)S(1)}, s32[32,40]{1,0:T(8,128)}, u32[]{:S(2)}) copy-start(s32[32,40]{1,0:T(8,128)} %down.1) | copy-start | bytes 15364
  99.2 7.7 %copy-start.18 = (f32[40]{0:T(128)S(1)}, f32[40]{0:T(128)}, u32[]{:S(2)}) copy-start(f32[40]{0:T(128)} %param.22) | copy-start | bytes 484
  99.2 7.7 %copy-start.19 = (f32[40]{0:T(128)S(1)}, f32[40]{0:T(128)}, u32[]{:S(2)}) copy-start(f32[40]{0:T(128)} %param.23) | copy-start | bytes 484
  99.3 0.7 copy-start.5
where the time goes:
time: 108 us; the launch traced here: 107 us
  Pallas kernels  58.3 us (54%)
  starting transfers between devices  25.1 us (23%)
  waiting for transfers between devices  18.1 us (17%)
  local copies, waits for them, and re-layouts  4.45 us (4%)
  between operations  1.09 us (1%)
    pallas_call x2, Pallas kernels, step(): call(functools.partial(commutator_kernel, min(size.unroll, 2), section, s...  17.3 us
    all_to_all x2, waiting for transfers between devices, step(): lax.all_to_all(send.reshape(N, 1, size.pieces * 128), 'ha', split_axis=0,...  16.7 us
    all_to_all x2, starting transfers between devices, step(): lax.all_to_all(send.reshape(N, 1, size.pieces * 128), 'ha', split_axis=0,...  16.1 us
    pallas_call x2, Pallas kernels, step(): call(functools.partial(place_kernel, min(size.unroll, 8), scale), [VMEM,...  11.7 us
    all_to_all x2, starting transfers between devices, step(): lax.all_to_all(relay.reshape(size.group, size.forward, WIDE), 'ha', split...  9.07 us
    pallas_call x1, Pallas kernels, begin(): call(functools.partial(open_kernel, size), [VMEM] * 6 + [HBM], [big, ((N...  9.01 us
    pallas_call x1, Pallas kernels, finish(): call(functools.partial(middle_kernel, size), [VMEM, VMEM, HBM, HBM, VMEM,...  7.57 us
    pallas_call x1, Pallas kernels, finish(): call(functools.partial(close_kernel, size), [VMEM, VMEM, HBM], [((A, 2 *...  6.88 us
  transfers between devices with their start and end apart: 4, of which 3 were waited for; matrix products, arithmetic and copies ran while one was open for 1% of the time, Pallas kernels for 27%

commit v1 on v0

--- a/solution.py
+++ b/solution.py
@@ -288,7 +288,7 @@
             for h in range(2):
                 state[h, pl.ds(2 * m + j, A, stride=ROWS), :] = pieces[2 * j + h]
 
-    each(0, M // 2, size.unroll, unfold)
+    each(0, M // 2, size.unroll * 6, unfold)
     give = parts(state, out, leave)
     for copy in give:
         copy.start()
@@ -369,7 +369,7 @@
     for r in range(size.slots):
         here = jnp.max(place[r * kinds : (r + 1) * kinds], axis=0, keepdims=True).astype(i32)
         ones[:, r * N : (r + 1) * N] = onehot(order == here)
-    lost[...] = jnp.broadcast_to(failed, (8, 128))
+    lost[...] = failed
     out = dot(ones[...], high[...]) + dot(ones[...], low[...])
     mine[...] = out[0:LIST]
     out = out[LIST:]
@@ -476,7 +476,7 @@
         give[j].start()
         each(j * PART, (j + 1) * PART, size.unroll, lambda a: table_aux(aux(middle, a), rows, a, table))
     choose.wait()
-    fill(size, table, chosen, slots, jnp.maximum(slots[4:5, 0:1], lost[0:1, 0:1].astype(f32)), send)
+    fill(size, table, chosen, slots, jnp.maximum(slots[4:5, 0:1], lost[...].astype(f32)), send)
     for copy in give:
         copy.wait()
 
@@ -500,7 +500,7 @@
             for i, piece in enumerate(narrow(*pieces)):
                 matrix[span, lanes(m * 384 + i * 128)] = piece
 
-        each(0, M // 2, size.unroll, fold)
+        each(0, M // 2, size.unroll * 6, fold)
         give.append(pltpu.make_async_copy(matrix.at[span, :], out.at[span, :], leave.at[j]))
         give[j].start()
     for copy in give:
@@ -568,7 +568,7 @@
             send.reshape(N, 1, size.pieces * 128), "ha", split_axis=0, concat_axis=0, tiled=True
         )
         base = call(
-            functools.partial(commutator_kernel, min(size.unroll, 2), section, scale),
+            functools.partial(commutator_kernel, min(size.unroll, 1), section, scale),
             [SMEM, SMEM] + [VMEM] * 4 + [HBM] * 2,
             [big],
             [big, big, big, ((256, 256), f32), ((A, 128), f32), sems, sems, sems],
@@ -579,7 +579,7 @@
         mine, relay, lost = call(
             functools.partial(receive_kernel, size),
             [VMEM],
-            [((LIST, WIDE), f32), ((size.relay, WIDE), f32), ((8, 128), i32)],
+            [((LIST, WIDE), f32), ((size.relay, WIDE), f32), ((1, 1), i32)],
             [ahead, ahead, ((LIST + size.relay, size.slots * N), bf16)],
             [VMEM, VMEM, VMEM],
         )(got.reshape(N * size.pieces, 128))
@@ -615,7 +615,7 @@
             [((A, 2 * M * M), f32)],
             [big, ((A, 2 * M * M), f32), sems, sems],
             [HBM],
-        )(pig, relay, partial)[0], lost[0, 0]
+        )(pig, relay, partial)[0], lost.reshape(())
 
     state, send, listed, slots = begin(MOST)
     relay, partial, lost = step(MOST, 0, HALF, state, state, send)

time: 108 us -> 106 us (0.981)
  waiting for transfers between devices: 18.1 us -> 13.6 us
  Pallas kernels: 58.3 us -> 62.1 us
  local copies, waits for them, and re-layouts: 4.45 us -> 3.29 us
    all_to_all x2, waiting for transfers between devices: 16.7 us -> 11.7 us  [step(): lax.all_to_all(send.reshape(N, 1, size.pieces * 128), 'ha', split_axis=0,...]
    pallas_call x2, Pallas kernels: 17.3 us -> 22.4 us  [step(): call(functools.partial(commutator_kernel, min(size.unroll, 1), section, s...]
    pallas_call x1, Pallas kernels: 6.88 us -> 5.36 us  [finish(): call(functools.partial(close_kernel, size), [VMEM, VMEM, HBM], [((A, 2 *...]
    slice x1 -> x0, local copies, waits for them, and re-layouts: 1.17 us -> none  [finish(): lost[0, 0]]
  transfers between devices with their start and end apart: 4 -> 4, of which waited for: 3 -> 4; matrix products, arithmetic and copies ran while one was open for 1% -> 0% of each run, Pallas kernels for 27% -> 32%
where the time goes in v1:
time: 106 us; the launch traced here: 105 us
  Pallas kernels  62.1 us (59%)
  starting transfers between devices  25.2 us (24%)
  waiting for transfers between devices  13.6 us (13%)
  local copies, waits for them, and re-layouts  3.29 us (3%)
  between operations  1.11 us (1%)
    pallas_call x2, Pallas kernels, step(): call(functools.partial(commutator_kernel, min(size.unroll, 1), section, s...  22.4 us
    all_to_all x2, starting transfers between devices, step(): lax.all_to_all(send.reshape(N, 1, size.pieces * 128), 'ha', split_axis=0,...  16.1 us
    pallas_call x2, Pallas kernels, step(): call(functools.partial(place_kernel, min(size.unroll, 8), scale), [VMEM,...  11.7 us
    all_to_all x2, waiting for transfers between devices, step(): lax.all_to_all(send.reshape(N, 1, size.pieces * 128), 'ha', split_axis=0,...  11.7 us
    all_to_all x2, starting transfers between devices, step(): lax.all_to_all(relay.reshape(size.group, size.forward, WIDE), 'ha', split...  9.08 us
    pallas_call x1, Pallas kernels, begin(): call(functools.partial(open_kernel, size), [VMEM] * 6 + [HBM], [big, ((N...  8.63 us
    pallas_call x1, Pallas kernels, finish(): call(functools.partial(middle_kernel, size), [VMEM, VMEM, HBM, HBM, VMEM,...  8.17 us
    pallas_call x2, Pallas kernels, step(): call(functools.partial(receive_kernel, size), [VMEM], [((LIST, WIDE), f32...  5.85 us
  transfers between devices with their start and end apart: 4, of which 4 were waited for; matrix products, arithmetic and copies ran while one was open for 0% of the time, Pallas kernels for 32%

profile of v1, /device:TPU:1, one launch (start us, length us, event | category | flops | bytes accessed | tf_op | source)
XLA Modules:
  0.0 105.3 jit_solution(10926167703830452403)
XLA Ops:
  0.0 0.0 copy-start.9
  0.0 0.0 copy-start.16
  0.0 0.0 copy-start.15
  0.0 0.0 copy-start.8
  0.0 0.0 copy-start.7
  0.0 0.0 copy-start.17
  0.0 8.6 %shard_map.120 = (f32[2,3104,128]{2,1,0:T(8,128)}, f32[1664,128]{1,0:T(8,128)}, bf16[192,1280]{1,0:T(8,128)(2,1)}, f32[8,192]{1,0:T(8,128)}) custom-call(s32[1,40]{1,0:T(1,128)} %bitcast.40, f32[1,40]{1,0:T(1,128)} %bitcast.50, f32[1,40]{1,0:T(1,128)} %bitcast.52, s32[32,40]{1,0:T(8,128)} %up.1, s32[32,40]{1,0:T(8,128)} %down.1, s32[32,40]{1,0:T(8,128)} %level.5, ...), custom_call_target="tpu_custom_call" | custom-call | tf_op jit(solution)/shard_map/pallas_call | solution.py:542
  8.7 11.5 %all-to-all-start.4 = ((f32[128,1,1664]{2,1,0:T(1,128)}), f32[128,1,1664]{2,1,0:T(1,128)S(1)}, u32[]{:S(2)}, u32[]{:S(2)}) async-start(f32[128,1,1664]{2,1,0:T(1,128)} %bitcast.33), calls=%async_computation.4 | async-start | bytes 1703936 | tf_op jit(solution)/shard_map/all_to_all | solution.py:567
  20.2 0.0 copy-done.9
  20.2 0.0 copy-done.16
  20.2 0.0 copy-done.15
  20.2 0.0 copy-done.8
  20.2 0.0 copy-done.7
  20.2 0.0 copy-done.17
  20.2 0.0 copy-start.14
  20.3 11.3 %shard_map.121.base = f32[2,3104,128]{2,1,0:T(8,128)} custom-call(f32[64]{0:T(128)S(1)} %copy-done.15, s32[2]{0:T(128)S(1)} %copy-done.16, f32[1,40]{1,0:T(1,128)S(1)} %bitcast.46, s32[32,40]{1,0:T(8,128)S(1)} %copy-done.9, f32[96,96]{1,0:T(8,128)S(1)} %copy-done.7, f32[96,96]{1,0:T(8,128)S(1)} %copy-done.8, f32[2,3104,128]{2,1,0:T(8,128)} %get-tuple-element.77.first.now, ...), custom_call_target="tpu_custom_call" | custom-call | tf_op jit(solution)/shard_map/pallas_call | solution.py:570
  31.5 5.7 %all-to-all-done.4 = f32[128,1,1664]{2,1,0:T(1,128)S(1)} async-done(((f32[128,1,1664]{2,1,0:T(1,128)}), f32[128,1,1664]{2,1,0:T(1,128)S(1)}, u32[]{:S(2)}, u32[]{:S(2)}) %all-to-all-start.4) | async-done | bytes 852000 | tf_op jit(solution)/shard_map/all_to_all | solution.py:567
  37.2 0.0 copy-start.4
  37.2 0.9 copy-done.4
  38.1 2.9 %shard_map.122 = (f32[192,512]{1,0:T(8,128)}, f32[128,512]{1,0:T(8,128)}, s32[1,1]{1,0:T(1,128)}) custom-call(f32[1664,128]{1,0:T(8,128)} %bitcast.27), custom_call_target="tpu_custom_call" | custom-call | tf_op jit(solution)/shard_map/pallas_call | solution.py:579
  41.0 4.5 %all-to-all-start.5 = ((f32[16,8,512]{2,1,0:T(8,128)}), f32[16,8,512]{2,1,0:T(8,128)S(1)}, u32[]{:S(2)}, u32[]{:S(2)}) async-start(f32[16,8,512]{2,1,0:T(8,128)} %bitcast.37), calls=%async_computation.5 | async-start | bytes 524288 | tf_op jit(solution)/shard_map/all_to_all | solution.py:586
  45.6 0.0 copy-done.14
  45.6 5.9 %shard_map.123.partial = f32[2,3104,128]{2,1,0:T(8,128)} custom-call(s32[1,40]{1,0:T(1,128)S(1)} %bitcast.41, f32[192,512]{1,0:T(8,128)} %get-tuple-element.80.mine, f32[2,3104,128]{2,1,0:T(8,128)} %shard_map.121.base), custom_call_target="tpu_custom_call" | custom-call | tf_op jit(solution)/shard_map/pallas_call | solution.py:594
  51.5 1.3 %all-to-all-done.5 = f32[16,8,512]{2,1,0:T(8,128)S(1)} async-done(((f32[16,8,512]{2,1,0:T(8,128)}), f32[16,8,512]{2,1,0:T(8,128)S(1)}, u32[]{:S(2)}, u32[]{:S(2)}) %all-to-all-start.5) | async-done | bytes 262176 | tf_op jit(solution)/shard_map/all_to_all | solution.py:586
  52.8 0.0 copy-start.5
  52.8 0.7 copy-done.5
  53.5 8.2 %shard_map.124 = (f32[2,3104,128]{2,1,0:T(8,128)}, f32[1664,128]{1,0:T(8,128)}) custom-call(s32[1,40]{1,0:T(1,128)S(1)} %bitcast.42, f32[128,512]{1,0:T(8,128)} %bitcast.30, f32[2,3104,128]{2,1,0:T(8,128)} %shard_map.123.partial, bf16[192,1280]{1,0:T(8,128)(2,1)} %get-tuple-element.82.listed, f32[8,192]{1,0:T(8,128)} %get-tuple-element.83.slots, ...), custom_call_target="tpu_custom_call" | custom-call | tf_op jit(solution)/shard_map/pallas_call | solution.py:604
  61.7 4.6 %all-to-all-start.6 = ((f32[128,1,1664]{2,1,0:T(1,128)}), f32[128,1,1664]{2,1,0:T(1,128)S(1)}, u32[]{:S(2)}, u32[]{:S(2)}) async-start(f32[128,1,1664]{2,1,0:T(1,128)} %bitcast.32), calls=%async_computation.6 | async-start | bytes 1703936 | tf_op jit(solution)/shard_map/all_to_all | solution.py:567
  66.3 11.1 %shard_map.125.base = f32[2,3104,128]{2,1,0:T(8,128)} custom-call(f32[64]{0:T(128)S(1)} %copy-done.15, s32[2]{0:T(128)S(1)} %copy-done.16, f32[1,40]{1,0:T(1,128)S(1)} %bitcast.47, s32[32,40]{1,0:T(8,128)S(1)} %copy-done.9, f32[96,96]{1,0:T(8,128)S(1)} %copy-done.7, f32[96,96]{1,0:T(8,128)S(1)} %copy-done.8, f32[2,3104,128]{2,1,0:T(8,128)} %get-tuple-element.77.first.now, ...), custom_call_target="tpu_custom_call" | custom-call | tf_op jit(solution)/shard_map/pallas_call | solution.py:570
  77.4 6.0 %all-to-all-done.6 = f32[128,1,1664]{2,1,0:T(1,128)S(1)} async-done(((f32[128,1,1664]{2,1,0:T(1,128)}), f32[128,1,1664]{2,1,0:T(1,128)S(1)}, u32[]{:S(2)}, u32[]{:S(2)}) %all-to-all-start.6) | async-done | bytes 852000 | tf_op jit(solution)/shard_map/all_to_all | solution.py:567
  83.4 0.0 copy-start.3
  83.4 0.9 copy-done.3
  84.3 2.9 %shard_map.126 = (f32[192,512]{1,0:T(8,128)}, f32[128,512]{1,0:T(8,128)}, s32[1,1]{1,0:T(1,128)}) custom-call(f32[1664,128]{1,0:T(8,128)} %bitcast.26), custom_call_target="tpu_custom_call" | custom-call | tf_op jit(solution)/shard_map/pallas_call | solution.py:579
  87.2 4.5 %all-to-all-start.7 = ((f32[16,8,512]{2,1,0:T(8,128)}), f32[16,8,512]{2,1,0:T(8,128)S(1)}, u32[]{:S(2)}, u32[]{:S(2)}) async-start(f32[16,8,512]{2,1,0:T(8,128)} %bitcast.36), calls=%async_computation.7 | async-start | bytes 524288 | tf_op jit(solution)/shard_map/all_to_all | solution.py:586
  92.4 5.8 %shard_map.127.partial = f32[2,3104,128]{2,1,0:T(8,128)} custom-call(s32[1,40]{1,0:T(1,128)S(1)} %bitcast.43, f32[192,512]{1,0:T(8,128)} %get-tuple-element.90.mine, f32[2,3104,128]{2,1,0:T(8,128)} %shard_map.125.base), custom_call_target="tpu_custom_call" | custom-call | tf_op jit(solution)/shard_map/pallas_call | solution.py:594
  98.3 0.0 copy-start
  98.3 0.0 copy-start.12
  98.3 0.0 copy-start.13
  98.3 0.0 copy-start.18
  98.3 0.0 copy-start.19
  98.3 0.7 all-to-all-done.7
  99.0 0.7 copy-done.6
  99.7 5.4 %shard_map.128 = f32[32,18432]{1,0:T(8,128)} custom-call(s32[1,40]{1,0:T(1,128)S(1)} %bitcast.44, f32[128,512]{1,0:T(8,128)} %bitcast.31, f32[2,3104,128]{2,1,0:T(8,128)} %shard_map.127.partial), custom_call_target="tpu_custom_call" | custom-call | tf_op jit(solution)/shard_map/pallas_call | solution.py:612
  105.1 0.0 copy-done
  105.1 0.0 copy-done.12
  105.1 0.0 copy-done.13
  105.1 0.0 copy-done.18
  105.1 0.0 copy-done.19
  (2 shorter events, 0.0 us)
Async XLA Ops:
  0.0 20.2 %copy-start.9 = (s32[32,40]{1,0:T(8,128)S(1)}, s32[32,40]{1,0:T(8,128)}, u32[]{:S(2)}) copy-start(s32[32,40]{1,0:T(8,128)} %level.5) | copy-start | bytes 15364
  0.0 20.2 %copy-start.16 = (s32[2]{0:T(128)S(1)}, s32[2]{0:T(128)}, u32[]{:S(2)}) copy-start(s32[2]{0:T(128)} %steps.3) | copy-start | bytes 28
  0.0 20.2 %copy-start.15 = (f32[64]{0:T(128)S(1)}, f32[64]{0:T(128)}, u32[]{:S(2)}) copy-start(f32[64]{0:T(128)} %field.3) | copy-start | bytes 772
  0.0 20.2 %copy-start.8 = (f32[96,96]{1,0:T(8,128)S(1)}, f32[96,96]{1,0:T(8,128)}, u32[]{:S(2)}) copy-start(f32[96,96]{1,0:T(8,128)} %dipole.3) | copy-start | bytes 110596
  0.0 20.2 %copy-start.7 = (f32[96,96]{1,0:T(8,128)S(1)}, f32[96,96]{1,0:T(8,128)}, u32[]{:S(2)}) copy-start(f32[96,96]{1,0:T(8,128)} %hamiltonian.3) | copy-start | bytes 110596
  0.0 20.2 %copy-start.17 = (f32[40]{0:T(128)S(1)}, f32[40]{0:T(128)}, u32[]{:S(2)}) copy-start(f32[40]{0:T(128)} %param.21) | copy-start | bytes 484
  8.7 28.6 %all-to-all-start.4 = ((f32[128,1,1664]{2,1,0:T(1,128)}), f32[128,1,1664]{2,1,0:T(1,128)S(1)}, u32[]{:S(2)}, u32[]{:S(2)}) async-start(f32[128,1,1664]{2,1,0:T(1,128)} %bitcast.33), calls=%async_computation.4 | async-start | bytes 1703936 | tf_op jit(solution)/shard_map/all_to_all | solution.py:567
  20.2 25.3 %copy-start.14 = (s32[40]{0:T(128)S(1)}, s32[40]{0:T(128)}, u32[]{:S(2)}) copy-start(s32[40]{0:T(128)} %param.18) | copy-start | bytes 484
  37.2 0.9 copy-start.4
  41.0 11.8 %all-to-all-start.5 = ((f32[16,8,512]{2,1,0:T(8,128)}), f32[16,8,512]{2,1,0:T(8,128)S(1)}, u32[]{:S(2)}, u32[]{:S(2)}) async-start(f32[16,8,512]{2,1,0:T(8,128)} %bitcast.37), calls=%async_computation.5 | async-start | bytes 524288 | tf_op jit(solution)/shard_map/all_to_all | solution.py:586
  52.8 0.7 copy-start.5
  61.7 21.7 %all-to-all-start.6 = ((f32[128,1,1664]{2,1,0:T(1,128)}), f32[128,1,1664]{2,1,0:T(1,128)S(1)}, u32[]{:S(2)}, u32[]{:S(2)}) async-start(f32[128,1,1664]{2,1,0:T(1,128)} %bitcast.32), calls=%async_computation.6 | async-start | bytes 1703936 | tf_op jit(solution)/shard_map/all_to_all | solution.py:567
  83.4 0.9 copy-start.3
  87.2 11.8 %all-to-all-start.7 = ((f32[16,8,512]{2,1,0:T(8,128)}), f32[16,8,512]{2,1,0:T(8,128)S(1)}, u32[]{:S(2)}, u32[]{:S(2)}) async-start(f32[16,8,512]{2,1,0:T(8,128)} %bitcast.36), calls=%async_computation.7 | async-start | bytes 524288 | tf_op jit(solution)/shard_map/all_to_all | solution.py:586
  98.3 6.8 %copy-start = (f32[32,18432]{1,0:T(8,128)S(1)}, f32[32,18432]{1,0:T(8,128)}, u32[]{:S(2)}) copy-start(f32[32,18432]{1,0:T(8,128)} %density.1) | copy-start | bytes 7077892
  98.3 6.8 %copy-start.12 = (s32[32,40]{1,0:T(8,128)S(1)}, s32[32,40]{1,0:T(8,128)}, u32[]{:S(2)}) copy-start(s32[32,40]{1,0:T(8,128)} %up.1) | copy-start | bytes 15364
  98.3 6.8 %copy-start.13 = (s32[32,40]{1,0:T(8,128)S(1)}, s32[32,40]{1,0:T(8,128)}, u32[]{:S(2)}) copy-start(s32[32,40]{1,0:T(8,128)} %down.1) | copy-start | bytes 15364
  98.3 6.8 %copy-start.18 = (f32[40]{0:T(128)S(1)}, f32[40]{0:T(128)}, u32[]{:S(2)}) copy-start(f32[40]{0:T(128)} %param.22) | copy-start | bytes 484
  98.3 6.8 %copy-start.19 = (f32[40]{0:T(128)S(1)}, f32[40]{0:T(128)}, u32[]{:S(2)}) copy-start(f32[40]{0:T(128)} %param.23) | copy-start | bytes 484
  99.0 0.7 copy-start.6
